TPU v7x, 256 devices: a whole 4x4x8 slice. The times are simulated.
256 devices in a mesh: blk: 32 (over z, x_lo, core), inner: 8 (over y, x_hi).
Axes of the slice: x: 4 (x_hi: 2, x_lo: 2; x = x_hi * 2 + x_lo), y: 4, z: 8, core: 2. Of those that a mesh axis runs over, the one named last changes fastest.
Arguments:
- echo_vectors: bfloat16 [32768, 768], P(('blk', 'inner')), may hold values from -9 to 9
- footage_vectors: bfloat16 [32768, 768], P(('blk', 'inner')), may hold values from -9 to 9
- match_numbers: int32 [32768], P(('blk', 'inner')), may hold values from 0 to 8191, as said below
- sharpness_factor: float32 [1], replicated, may hold values from 30 to 50
- score_offset: float32 [1], replicated, may hold values from -11 to -9
Outputs:
- grad_image: bfloat16 [32768, 768], P(('blk', 'inner'))
- grad_text: bfloat16 [32768, 768], P(('blk', 'inner'))
- loss: float32 [1], replicated
Inputs may be any that keep to these rules, and one draw needn't show every extreme that they name: `match_numbers`: at most 8192 distinct ids; clips that share an id form positive pairs.
All inputs are finite; a program needn't handle non-finite values.
Results may differ from a plain program's by a relative error of at most 0.013.
Values may be sent and summed in bfloat16 or wider, within the bound.
A program may use at most 64 MiB of HBM per device.

v0:
```python
import jax
import jax.numpy as jnp
from jax import lax
from jax.sharding import PartitionSpec as P


def from_behind(value, axis, by):
    size = lax.axis_size(axis)
    return lax.ppermute(value, axis, [(i, (i + by) % size) for i in range(size)])


def normalize(raw):
    values = raw.astype(jnp.float32)
    row_norm = jnp.sqrt(jnp.sum(values * values, axis=-1, keepdims=True) + 1e-06)
    return (values / row_norm, row_norm)


def unit_back(unit_f32, row_norm, unit_grad):
    inner_prod = jnp.sum(unit_f32 * unit_grad, axis=-1, keepdims=True)
    return ((unit_grad - unit_f32 * inner_prod) / row_norm).astype(jnp.bfloat16)


def meet_block(image_rows, image_ids, caption_vectors, text_ids, score_factor, logit_bias):
    logits = (
        score_factor
        * lax.dot_general(
            caption_vectors,
            image_rows,
            (((1,), (1,)), ((), ())),
            preferred_element_type=jnp.float32,
        )
        + logit_bias
    )
    label_sign = jnp.where(text_ids[:, None] == image_ids[None, :], 1.0, -1.0).astype(jnp.float32)
    loss_part = jnp.sum(jax.nn.log_sigmoid(label_sign * logits))
    weights = (-label_sign * jax.nn.sigmoid(-label_sign * logits) * score_factor).astype(
        jnp.bfloat16
    )
    text_part = jnp.dot(weights, image_rows, preferred_element_type=jnp.float32)
    image_part = lax.dot_general(
        weights, caption_vectors, (((0,), (0,)), ((), ())), preferred_element_type=jnp.float32
    )
    return (loss_part, text_part, image_part)


def per_device(echo_vectors, footage_vectors, match_numbers, sharpness_factor, score_offset):
    score_factor = sharpness_factor[0]
    logit_bias = score_offset[0]
    image_f32, image_norm = normalize(echo_vectors)
    text_f32, text_norm = normalize(footage_vectors)
    image_unit = image_f32.astype(jnp.bfloat16)
    text_unit = text_f32.astype(jnp.bfloat16)
    group_rows, group_ids = (
        lax.all_gather(image_unit, "inner", axis=0, tiled=True),
        lax.all_gather(match_numbers, "inner", axis=0, tiled=True),
    )
    cycle_size = lax.axis_size("blk")
    image_grad = jnp.zeros(group_rows.shape, jnp.float32)
    loss_sum = jnp.zeros((), jnp.float32)
    empty_grad = jnp.zeros(text_unit.shape, jnp.float32)

    def absorb(image_grad, loss_sum, caption_vectors, text_ids, video_embedding_gradient):
        loss_part, text_part, image_part = meet_block(
            group_rows, group_ids, caption_vectors, text_ids, score_factor, logit_bias
        )
        return (image_grad + image_part, loss_sum + loss_part, video_embedding_gradient + text_part)

    def advance(index_now, loop_state):
        image_grad, loss_sum, caption_vectors, text_ids, video_embedding_gradient = loop_state
        image_grad, loss_sum, video_embedding_gradient = absorb(
            image_grad, loss_sum, caption_vectors, text_ids, video_embedding_gradient
        )
        caption_vectors, text_ids, video_embedding_gradient = (
            from_behind(caption_vectors.astype(jnp.float32), "blk", 1).astype(
                caption_vectors.dtype
            ),
            from_behind(text_ids, "blk", 1),
            from_behind(video_embedding_gradient, "blk", 1),
        )
        return (image_grad, loss_sum, caption_vectors, text_ids, video_embedding_gradient)

    start = (image_grad, loss_sum, text_unit, match_numbers, empty_grad)
    image_grad, loss_sum, caption_vectors, text_ids, text_home = lax.fori_loop(
        0, cycle_size, advance, start
    )
    own_image = lax.psum_scatter(
        image_grad.astype(jnp.bfloat16), "inner", scatter_dimension=0, tiled=True
    ).astype(jnp.float32)
    loss_all = lax.psum(loss_sum, ("blk", "inner"))
    batch_total = text_unit.shape[0] * cycle_size * lax.axis_size("inner")
    loss = (-loss_all / batch_total).reshape(1)
    grad_image = unit_back(image_f32, image_norm, own_image)
    grad_text = unit_back(text_f32, text_norm, text_home)
    return (grad_image, grad_text, loss)


def solution(mesh):
    return jax.shard_map(
        per_device,
        mesh=mesh,
        in_specs=(
            P(("blk", "inner"), None),
            P(("blk", "inner"), None),
            P(("blk", "inner")),
            P(),
            P(),
        ),
        out_specs=(P(("blk", "inner"), None), P(("blk", "inner"), None), P()),
        check_vma=False,
    )
```

profile of v0, /device:TPU:1, one launch (start us, length us, event | category | flops | bytes accessed | tf_op | source)
XLA Modules:
  0.0 757.1 jit_solution(12758062524664124846)
XLA Ops:
  11.3 20.8 %all-gather = s32[8,1,128]{2,1,0:T(1,128)S(1)} all-gather(s32[1,1,128]{2,1,0:T(1,128)} %bitcast), channel_id=1, replica_groups=mesh['blk'=32,'inner'=8] {'inner'}, dimensions={0}, use_global_device_ids=true | all-gather | bytes 4608 | tf_op jit(solution)/shard_map/all_gather | solution.py:55
  34.2 35.2 %all-gather.3.cloned.1.call-done = bf16[1024,768]{1,0:T(8,128)(2,1)} async-done(((bf16[128,768]{1,0:T(8,128)(2,1)}), bf16[1024,768]{1,0:T(8,128)(2,1)}) %all-gather.3.cloned.1.call-update) | async-done | bytes 1572880 | tf_op jit(solution)/shard_map/all_gather | solution.py:54
  70.1 592.2 %while.19 = (s32[]{:T(128)}, f32[1024,768]{1,0:T(8,128)S(1)}, f32[]{:T(128)}, bf16[128,768]{1,0:T(8,128)(2,1)S(1)}, s32[128]{0:T(128)}, /*index=5*/f32[128,768]{...) while((s32[]{:T(128)}, f32[1024,768]{1,0:T(8,128)S(1)}, ...), condition=%wide.region_4.5_spmd.clone, body=%wide.region_2.4_spmd.clone.sunk | while | flops 609976320 | bytes 23348056 | solution.py:83
  72.2 4.2 fusion.37
  109.1 4.2 fusion.37
  128.0 4.2 fusion.37
  146.0 4.2 fusion.37
  164.9 4.2 fusion.37
  183.2 4.2 fusion.37
  203.0 4.2 fusion.37
  222.1 4.2 fusion.37
  240.6 4.2 fusion.37
  259.1 4.2 fusion.37
  277.5 4.2 fusion.37
  296.0 4.2 fusion.37
  314.5 4.2 fusion.37
  333.0 4.2 fusion.37
  351.5 4.2 fusion.37
  370.0 4.2 fusion.37
  406.9 4.2 fusion.37
  425.4 4.2 fusion.37
  443.9 4.2 fusion.37
  462.4 4.2 fusion.37
  663.7 78.8 %psum.7 = f32[]{:T(128)} all-reduce(f32[]{:T(128)} %get-tuple-element.59), channel_id=1, replica_groups=mesh['blk'=32,'inner'=8] {'blk','inner'}, use_global_device_ids=true, to_apply=%region_8.9 | all-reduce | flops 1 | bytes 8 | tf_op jit(solution)/shard_map/psum | solution.py:89
  (483 shorter events, 500.3 us)
Async XLA Ops:
  7.2 62.2 %all-gather.3.cloned.1.call-start = ((), (), s32[]{:S(2)}) async-start(), calls=%async_computation.1 | async-start | bytes 1769472 | tf_op jit(solution)/shard_map/all_gather | solution.py:54
  11.2 734.9 %reduce-scatter.2.cloned.1.call-start = ((), (), s32[]{:S(2)}) async-start(), calls=%async_computation.2 | async-start | bytes 1769472 | tf_op jit(solution)/shard_map/reduce_scatter | solution.py:86
  106.5 16.7 %collective-permute-start.1 = (s32[128]{0:T(128)S(1)}, s32[128]{0:T(128)}, u32[]{:S(2)}, u32[]{:S(2)}) collective-permute-start(s32[128]{0:T(128)S(1)} %copy.18), channel_id=1, source_target_pairs={{0,8},{8,16},{16,24},{24,32},{32,40},{40,48},{48,56},{56,64},{64,7... | collective-permute-start | bytes 1544 | tf_op jit(solution)/shard_map/while/body/eval_jaxpr/ppermute | solution.py:9
  143.4 16.7 %collective-permute-start.1 = (s32[128]{0:T(128)S(1)}, s32[128]{0:T(128)}, u32[]{:S(2)}, u32[]{:S(2)}) collective-permute-start(s32[128]{0:T(128)S(1)} %copy.18), channel_id=1, source_target_pairs={{0,8},{8,16},{16,24},{24,32},{32,40},{40,48},{48,56},{56,64},{64,7... | collective-permute-start | bytes 1544 | tf_op jit(solution)/shard_map/while/body/eval_jaxpr/ppermute | solution.py:9
  180.2 18.0 %collective-permute-start.1 = (s32[128]{0:T(128)S(1)}, s32[128]{0:T(128)}, u32[]{:S(2)}, u32[]{:S(2)}) collective-permute-start(s32[128]{0:T(128)S(1)} %copy.18), channel_id=1, source_target_pairs={{0,8},{8,16},{16,24},{24,32},{32,40},{40,48},{48,56},{56,64},{64,7... | collective-permute-start | bytes 1544 | tf_op jit(solution)/shard_map/while/body/eval_jaxpr/ppermute | solution.py:9
  200.4 16.9 %collective-permute-start.1 = (s32[128]{0:T(128)S(1)}, s32[128]{0:T(128)}, u32[]{:S(2)}, u32[]{:S(2)}) collective-permute-start(s32[128]{0:T(128)S(1)} %copy.18), channel_id=1, source_target_pairs={{0,8},{8,16},{16,24},{24,32},{32,40},{40,48},{48,56},{56,64},{64,7... | collective-permute-start | bytes 1544 | tf_op jit(solution)/shard_map/while/body/eval_jaxpr/ppermute | solution.py:9
  219.5 16.3 %collective-permute-start.1 = (s32[128]{0:T(128)S(1)}, s32[128]{0:T(128)}, u32[]{:S(2)}, u32[]{:S(2)}) collective-permute-start(s32[128]{0:T(128)S(1)} %copy.18), channel_id=1, source_target_pairs={{0,8},{8,16},{16,24},{24,32},{32,40},{40,48},{48,56},{56,64},{64,7... | collective-permute-start | bytes 1544 | tf_op jit(solution)/shard_map/while/body/eval_jaxpr/ppermute | solution.py:9
  238.0 16.3 %collective-permute-start.1 = (s32[128]{0:T(128)S(1)}, s32[128]{0:T(128)}, u32[]{:S(2)}, u32[]{:S(2)}) collective-permute-start(s32[128]{0:T(128)S(1)} %copy.18), channel_id=1, source_target_pairs={{0,8},{8,16},{16,24},{24,32},{32,40},{40,48},{48,56},{56,64},{64,7... | collective-permute-start | bytes 1544 | tf_op jit(solution)/shard_map/while/body/eval_jaxpr/ppermute | solution.py:9
  256.5 16.3 %collective-permute-start.1 = (s32[128]{0:T(128)S(1)}, s32[128]{0:T(128)}, u32[]{:S(2)}, u32[]{:S(2)}) collective-permute-start(s32[128]{0:T(128)S(1)} %copy.18), channel_id=1, source_target_pairs={{0,8},{8,16},{16,24},{24,32},{32,40},{40,48},{48,56},{56,64},{64,7... | collective-permute-start | bytes 1544 | tf_op jit(solution)/shard_map/while/body/eval_jaxpr/ppermute | solution.py:9
  275.0 16.3 %collective-permute-start.1 = (s32[128]{0:T(128)S(1)}, s32[128]{0:T(128)}, u32[]{:S(2)}, u32[]{:S(2)}) collective-permute-start(s32[128]{0:T(128)S(1)} %copy.18), channel_id=1, source_target_pairs={{0,8},{8,16},{16,24},{24,32},{32,40},{40,48},{48,56},{56,64},{64,7... | collective-permute-start | bytes 1544 | tf_op jit(solution)/shard_map/while/body/eval_jaxpr/ppermute | solution.py:9
  293.4 16.3 %collective-permute-start.1 = (s32[128]{0:T(128)S(1)}, s32[128]{0:T(128)}, u32[]{:S(2)}, u32[]{:S(2)}) collective-permute-start(s32[128]{0:T(128)S(1)} %copy.18), channel_id=1, source_target_pairs={{0,8},{8,16},{16,24},{24,32},{32,40},{40,48},{48,56},{56,64},{64,7... | collective-permute-start | bytes 1544 | tf_op jit(solution)/shard_map/while/body/eval_jaxpr/ppermute | solution.py:9
  311.9 16.3 %collective-permute-start.1 = (s32[128]{0:T(128)S(1)}, s32[128]{0:T(128)}, u32[]{:S(2)}, u32[]{:S(2)}) collective-permute-start(s32[128]{0:T(128)S(1)} %copy.18), channel_id=1, source_target_pairs={{0,8},{8,16},{16,24},{24,32},{32,40},{40,48},{48,56},{56,64},{64,7... | collective-permute-start | bytes 1544 | tf_op jit(solution)/shard_map/while/body/eval_jaxpr/ppermute | solution.py:9
  330.4 16.3 %collective-permute-start.1 = (s32[128]{0:T(128)S(1)}, s32[128]{0:T(128)}, u32[]{:S(2)}, u32[]{:S(2)}) collective-permute-start(s32[128]{0:T(128)S(1)} %copy.18), channel_id=1, source_target_pairs={{0,8},{8,16},{16,24},{24,32},{32,40},{40,48},{48,56},{56,64},{64,7... | collective-permute-start | bytes 1544 | tf_op jit(solution)/shard_map/while/body/eval_jaxpr/ppermute | solution.py:9
  348.9 16.3 %collective-permute-start.1 = (s32[128]{0:T(128)S(1)}, s32[128]{0:T(128)}, u32[]{:S(2)}, u32[]{:S(2)}) collective-permute-start(s32[128]{0:T(128)S(1)} %copy.18), channel_id=1, source_target_pairs={{0,8},{8,16},{16,24},{24,32},{32,40},{40,48},{48,56},{56,64},{64,7... | collective-permute-start | bytes 1544 | tf_op jit(solution)/shard_map/while/body/eval_jaxpr/ppermute | solution.py:9
  367.4 16.3 %collective-permute-start.1 = (s32[128]{0:T(128)S(1)}, s32[128]{0:T(128)}, u32[]{:S(2)}, u32[]{:S(2)}) collective-permute-start(s32[128]{0:T(128)S(1)} %copy.18), channel_id=1, source_target_pairs={{0,8},{8,16},{16,24},{24,32},{32,40},{40,48},{48,56},{56,64},{64,7... | collective-permute-start | bytes 1544 | tf_op jit(solution)/shard_map/while/body/eval_jaxpr/ppermute | solution.py:9
  385.9 16.3 %collective-permute-start.1 = (s32[128]{0:T(128)S(1)}, s32[128]{0:T(128)}, u32[]{:S(2)}, u32[]{:S(2)}) collective-permute-start(s32[128]{0:T(128)S(1)} %copy.18), channel_id=1, source_target_pairs={{0,8},{8,16},{16,24},{24,32},{32,40},{40,48},{48,56},{56,64},{64,7... | collective-permute-start | bytes 1544 | tf_op jit(solution)/shard_map/while/body/eval_jaxpr/ppermute | solution.py:9
  404.3 16.3 %collective-permute-start.1 = (s32[128]{0:T(128)S(1)}, s32[128]{0:T(128)}, u32[]{:S(2)}, u32[]{:S(2)}) collective-permute-start(s32[128]{0:T(128)S(1)} %copy.18), channel_id=1, source_target_pairs={{0,8},{8,16},{16,24},{24,32},{32,40},{40,48},{48,56},{56,64},{64,7... | collective-permute-start | bytes 1544 | tf_op jit(solution)/shard_map/while/body/eval_jaxpr/ppermute | solution.py:9
  422.8 16.3 %collective-permute-start.1 = (s32[128]{0:T(128)S(1)}, s32[128]{0:T(128)}, u32[]{:S(2)}, u32[]{:S(2)}) collective-permute-start(s32[128]{0:T(128)S(1)} %copy.18), channel_id=1, source_target_pairs={{0,8},{8,16},{16,24},{24,32},{32,40},{40,48},{48,56},{56,64},{64,7... | collective-permute-start | bytes 1544 | tf_op jit(solution)/shard_map/while/body/eval_jaxpr/ppermute | solution.py:9
  441.3 16.3 %collective-permute-start.1 = (s32[128]{0:T(128)S(1)}, s32[128]{0:T(128)}, u32[]{:S(2)}, u32[]{:S(2)}) collective-permute-start(s32[128]{0:T(128)S(1)} %copy.18), channel_id=1, source_target_pairs={{0,8},{8,16},{16,24},{24,32},{32,40},{40,48},{48,56},{56,64},{64,7... | collective-permute-start | bytes 1544 | tf_op jit(solution)/shard_map/while/body/eval_jaxpr/ppermute | solution.py:9
  459.8 16.3 %collective-permute-start.1 = (s32[128]{0:T(128)S(1)}, s32[128]{0:T(128)}, u32[]{:S(2)}, u32[]{:S(2)}) collective-permute-start(s32[128]{0:T(128)S(1)} %copy.18), channel_id=1, source_target_pairs={{0,8},{8,16},{16,24},{24,32},{32,40},{40,48},{48,56},{56,64},{64,7... | collective-permute-start | bytes 1544 | tf_op jit(solution)/shard_map/while/body/eval_jaxpr/ppermute | solution.py:9
  478.3 16.3 %collective-permute-start.1 = (s32[128]{0:T(128)S(1)}, s32[128]{0:T(128)}, u32[]{:S(2)}, u32[]{:S(2)}) collective-permute-start(s32[128]{0:T(128)S(1)} %copy.18), channel_id=1, source_target_pairs={{0,8},{8,16},{16,24},{24,32},{32,40},{40,48},{48,56},{56,64},{64,7... | collective-permute-start | bytes 1544 | tf_op jit(solution)/shard_map/while/body/eval_jaxpr/ppermute | solution.py:9
  496.8 16.3 %collective-permute-start.1 = (s32[128]{0:T(128)S(1)}, s32[128]{0:T(128)}, u32[]{:S(2)}, u32[]{:S(2)}) collective-permute-start(s32[128]{0:T(128)S(1)} %copy.18), channel_id=1, source_target_pairs={{0,8},{8,16},{16,24},{24,32},{32,40},{40,48},{48,56},{56,64},{64,7... | collective-permute-start | bytes 1544 | tf_op jit(solution)/shard_map/while/body/eval_jaxpr/ppermute | solution.py:9
  515.2 16.3 %collective-permute-start.1 = (s32[128]{0:T(128)S(1)}, s32[128]{0:T(128)}, u32[]{:S(2)}, u32[]{:S(2)}) collective-permute-start(s32[128]{0:T(128)S(1)} %copy.18), channel_id=1, source_target_pairs={{0,8},{8,16},{16,24},{24,32},{32,40},{40,48},{48,56},{56,64},{64,7... | collective-permute-start | bytes 1544 | tf_op jit(solution)/shard_map/while/body/eval_jaxpr/ppermute | solution.py:9
  533.7 16.3 %collective-permute-start.1 = (s32[128]{0:T(128)S(1)}, s32[128]{0:T(128)}, u32[]{:S(2)}, u32[]{:S(2)}) collective-permute-start(s32[128]{0:T(128)S(1)} %copy.18), channel_id=1, source_target_pairs={{0,8},{8,16},{16,24},{24,32},{32,40},{40,48},{48,56},{56,64},{64,7... | collective-permute-start | bytes 1544 | tf_op jit(solution)/shard_map/while/body/eval_jaxpr/ppermute | solution.py:9
  (140 other events, 1293.1 us)
Sparse Core Ops, SparseCore 0:
  11.4 57.9 all-gather.2
  663.8 77.7 reduce-scatter.1
where the time goes:
time: 763 us; the launch traced here: 757 us
  matrix products  323 us (42%)
  starting transfers between devices  151 us (20%)
  blocking collectives  99.6 us (13%)
  waiting for transfers between devices  79.5 us (10%)
  local copies, waits for them, and re-layouts  53.5 us (7%)
  loops' own time  22.3 us (3%)
  between operations  15.9 us (2%)
  other arithmetic  12.1 us (2%)
    ppermute x96, starting transfers between devices, from_behind(): lax.ppermute(value, axis, [(i, (i + by) % size) for i in range(size)])  151 us
    dot_general x32, matrix products, meet_block(): lax.dot_general(caption_vectors, image_rows, (((1,), (1,)), ((), ())), pr...  134 us
    dot_general x32, matrix products, meet_block(): lax.dot_general(weights, caption_vectors, (((0,), (0,)), ((), ())), prefe...  95.1 us
    dot_general x32, matrix products, meet_block(): text_part = jnp.dot(weights, image_rows, preferred_element_type=jnp.float32)  94.2 us
    psum x1, blocking collectives, per_device(): loss_all = lax.psum(loss_sum, ('blk', 'inner'))  78.8 us
    while x192, local copies, waits for them, and re-layouts  51.5 us
    ppermute x96, waiting for transfers between devices, from_behind(): lax.ppermute(value, axis, [(i, (i + by) % size) for i in range(size)])  44.3 us
    all_gather x1, waiting for transfers between devices, per_device(): lax.all_gather(image_unit, 'inner', axis=0, tiled=True)  35.2 us
  transfers between devices with their start and end apart: 98, of which 33 were waited for; matrix products, arithmetic and copies ran while one was open for 43% of the time, Pallas kernels for 0%

commit v1 on v0

v1 whole, which is shorter than its diff:
```python
import functools
import math

import jax
import jax.numpy as jnp
from jax import lax
from jax.experimental import pallas as pl
from jax.experimental.pallas import tpu as pltpu
from jax.sharding import PartitionSpec as P

ROWS, D = 128, 768
TILES = D // 128
BLOCK = D + 16
SLOTS = 16
N = SLOTS * ROWS
BATCH = 32768
MESH = pl.DeviceIdType.MESH

WHOLE, A, B = (0, BLOCK), (0, 384), (384, BLOCK)
A0, A1, B0, B1 = (0, 192), (192, 384), (384, 576), (576, BLOCK)

PLACES = [
    (0, 0), (1, 0), (3, 0), (0, 1), (0, 3),
    (2, 0), (0, 2), (1, 1), (1, 3), (3, 1), (3, 3),
    (2, 1), (2, 3), (1, 2), (3, 2), (2, 2),
]
ISLOT = {place: slot for slot, place in enumerate(PLACES)}
STEP = {"+x": (1, 0), "-x": (3, 0), "+y": (0, 1), "-y": (0, 3)}
BACK = {"+x": "-x", "-x": "+x", "+y": "-y", "-y": "+y", "+z": "-z", "-z": "+z"}
IMG = [
    [((0, 0), WHOLE, d) for d in ("+x", "-x", "+y", "-y")],
    [
        ((0, 1), B, "+x"), ((0, 1), B, "-x"), ((1, 0), A, "+y"), ((1, 0), A, "-y"),
        ((0, 3), B, "+x"), ((0, 3), B, "-x"), ((3, 0), A, "+y"), ((3, 0), A, "-y"),
        ((3, 0), A, "+x"), ((1, 0), B, "-x"), ((0, 3), A, "+y"), ((0, 1), B, "-y"),
    ],
    [
        ((0, 2), B, "+x"), ((0, 2), B, "-x"), ((2, 0), A, "+y"), ((2, 0), A, "-y"),
        ((3, 1), B0, "+x"), ((1, 1), B1, "-x"), ((1, 3), A0, "+y"), ((1, 1), A1, "-y"),
        ((3, 3), B0, "+x"), ((1, 3), B1, "-x"), ((3, 3), A0, "+y"), ((3, 1), A1, "-y"),
    ],
    [((3, 2), B0, "+x"), ((1, 2), B1, "-x"), ((2, 3), A0, "+y"), ((2, 1), A1, "-y")],
]
DZ = [0, 1, 7, 2, 6, 3, 5, 4]
TPLACE = {dz: k for k, dz in enumerate(DZ)}
TXT = [
    [(0, WHOLE, "+z"), (0, WHOLE, "-z")],
    [(7, WHOLE, "+z"), (1, WHOLE, "-z")],
    [(6, WHOLE, "+z"), (2, WHOLE, "-z")],
    [(5, A, "+z"), (3, B, "-z")],
]
FRESH = [[0], [1, 7], [2, 6], [3, 5], [4]]


def img_to(place, direction):
    sx, sy = STEP[direction]
    return ((place[0] - sx) % 4, (place[1] - sy) % 4)


def txt_to(dz, direction):
    return (dz - 1) % 8 if direction == "+z" else (dz + 1) % 8


def numbered(rounds, to, slot_of):
    gather, scatter, count, land = [], [], 0, 0
    for moves in rounds:
        out, back = [], []
        for place, (lo, hi), direction in moves:
            there = to(place, direction)
            out.append((count, slot_of[place], slot_of[there], lo, hi, direction))
            top = min(hi, D)
            back.append((count, slot_of[there], slot_of[place], lo, top, BACK[direction], land))
            land += top - lo
            count += 1
        gather.append(out)
        scatter.append(back)
    return gather, scatter, count, land


IMG_OUT, IMG_BACK, IMG_N, IMG_LAND = numbered(IMG, img_to, ISLOT)
TXT_OUT, TXT_BACK, TXT_N, TXT_LAND = numbered(TXT, txt_to, TPLACE)


def spans(lo, hi):
    parts = []
    while lo < hi:
        tile = lo // 128
        end = min(hi, (tile + 1) * 128)
        parts.append((tile, lo - tile * 128, end - tile * 128))
        lo = end
    return parts


def kernel(
    echo_ref, footage_ref, ids_ref, sharp_ref, offset_ref,
    gimg_ref, gtxt_ref, loss_ref,
    irx, trx, img, txt, idi, idt, gi, gt,
    isend, iland, tsend, tland, ssend, sland,
    total, lc, lx, ly, lz,
    ig_s, ig_r, tg_s, tg_r, sg_s, sg_r,
    is_s, is_r, ts_s, ts_r, ss_s, ss_r, l_s, l_r,
):
    blk, inner = lax.axis_index("blk"), lax.axis_index("inner")
    core = lax.rem(blk, 2)
    z = lax.div(blk, 4)
    x = lax.rem(inner, 2) * 2 + lax.rem(lax.div(blk, 2), 2)
    y = lax.div(inner, 2)

    def at(z, x, y, core):
        return {
            "blk": z * 4 + lax.rem(x, 2) * 2 + core,
            "inner": y * 2 + lax.div(x, 2),
        }

    xs = [at(z, lax.rem(x + k, 4), y, core) for k in range(4)]
    ys = [at(z, x, lax.rem(y + k, 4), core) for k in range(4)]
    zs = [at(lax.rem(z + k, 8), x, y, core) for k in range(8)]
    sib = at(z, x, y, 1 - core)
    near = {"+x": xs[1], "-x": xs[3], "+y": ys[1], "-y": ys[3], "+z": zs[1], "-z": zs[7]}

    barrier = pltpu.get_barrier_semaphore()
    partners = xs[1:] + ys[1:] + zs[1:] + [sib]
    for device in partners:
        pl.semaphore_signal(barrier, inc=1, device_id=device, device_id_type=MESH)

    def unit32(ref):
        values = ref[...].astype(jnp.float32)
        norm = jnp.sqrt(jnp.sum(values * values, axis=-1, keepdims=True) + 1e-06)
        return values / norm, norm

    ids = ids_ref[...]
    row = lax.broadcasted_iota(jnp.int32, (16, 128), 0)
    high = jnp.broadcast_to((ids >> 6).astype(jnp.float32), (16, 128))
    low = jnp.broadcast_to((ids & 63).astype(jnp.float32), (16, 128))
    id_rows = jnp.where(row == 0, high, jnp.where(row == 1, low, 0.0)).astype(jnp.bfloat16)
    for ref, slots in ((echo_ref, irx), (footage_ref, trx)):
        unit = unit32(ref)[0].astype(jnp.bfloat16)
        for c in range(TILES):
            slots[pl.ds(c * 128, 128), :] = unit[:, c * 128 : (c + 1) * 128]
        slots[pl.ds(D, 16), :] = id_rows

    pl.semaphore_wait(barrier, len(partners))

    def remote(src, dst, send, recv, device):
        return pltpu.make_async_remote_copy(
            src_ref=src, dst_ref=dst, send_sem=send, recv_sem=recv,
            device_id=device, device_id_type=MESH,
        )

    def img_copy(move):
        k, slot, there, lo, hi, direction = move
        return remote(
            irx.at[pl.ds(slot * BLOCK + lo, hi - lo)], irx.at[pl.ds(there * BLOCK + lo, hi - lo)],
            ig_s.at[k], ig_r.at[k], near[direction],
        )

    def txt_copy(move):
        k, slot, there, lo, hi, direction = move
        return remote(
            trx.at[pl.ds(slot * BLOCK + lo, hi - lo)], trx.at[pl.ds(there * BLOCK + lo, hi - lo)],
            tg_s.at[k], tg_r.at[k], near[direction],
        )

    def sib_copy(k):
        return remote(
            trx.at[pl.ds(k * BLOCK, BLOCK)], trx.at[pl.ds((8 + k) * BLOCK, BLOCK)],
            sg_s.at[k], sg_r.at[k], sib,
        )

    def img_start(r):
        for move in IMG_OUT[r]:
            img_copy(move).start()

    def img_wait(r):
        for move in IMG_OUT[r]:
            img_copy(move).wait_recv()

    def txt_start(r):
        if r < 4:
            for move in TXT_OUT[r]:
                txt_copy(move).start()
        for dz in FRESH[r]:
            sib_copy(TPLACE[dz]).start()

    def txt_wait(r):
        for move in TXT_OUT[r]:
            txt_copy(move).wait_recv()

    def sib_wait(r):
        for dz in FRESH[r]:
            sib_copy(TPLACE[dz]).wait_recv()

    def ids_of(slots, base):
        pair = slots[pl.ds(base + D, 16), :].astype(jnp.float32)
        return pair[0:1, :] * 64.0 + pair[1:2, :]

    def take_img(first, count):
        def body(s, carry):
            base = pl.multiple_of(s * BLOCK, 16)
            rows = pl.ds(pl.multiple_of(s * 128, 128), 128)
            for c in range(TILES):
                img[rows, c * 128 : (c + 1) * 128] = irx[pl.ds(base + c * 128, 128), :]
            idi[rows, :] = jnp.broadcast_to(ids_of(irx, base), (128, 128)).T
            return carry
        lax.fori_loop(first, first + count, body, 0)

    def take_txt(places, lane):
        for k in places:
            slot = 2 * k + lane
            base = (8 * lane + k) * BLOCK
            for c in range(TILES):
                txt[slot * 128 : (slot + 1) * 128, c * 128 : (c + 1) * 128] = trx[
                    pl.ds(base + c * 128, 128), :
                ]
            idt[:, slot * 128 : (slot + 1) * 128] = ids_of(trx, base)

    scale = sharp_ref[0] * (1.0 / math.log(2.0))
    shift = offset_ref[0] * (1.0 / math.log(2.0))

    def pairs(i0, ni, j0, nj):
        rows, cols = pl.ds(i0, ni), pl.ds(j0, nj)
        dots = lax.dot_general(
            img[rows, :], txt[cols, :], (((1,), (1,)), ((), ())),
            preferred_element_type=jnp.float32,
        )
        logits = dots * scale + shift
        match = jnp.concatenate([idi[rows, :]] * (nj // 128), axis=1) == idt[:, cols]
        power = jnp.exp2(jnp.where(match, -logits, logits))
        whole = 1.0 + power
        part = power * pl.reciprocal(whole, approx=True)
        weights = jnp.where(match, -part, part).astype(jnp.bfloat16)
        terms = jnp.log2(whole).reshape(ni // 8, 8, nj).sum(axis=0)
        total[...] += sum(terms[:, c * 128 : (c + 1) * 128] for c in range(nj // 128))
        gi[rows, :] += jnp.dot(weights, txt[cols, :], preferred_element_type=jnp.float32)
        gt[cols, :] += lax.dot_general(
            weights, img[rows, :], (((0,), (0,)), ((), ())),
            preferred_element_type=jnp.float32,
        )

    def pack(acc, block, out, base, lo, hi):
        for tile, first, end in spans(lo, hi):
            out[pl.ds(base + tile * 128 + first, end - first), :] = acc[
                pl.ds(block * 128 + first, end - first), tile * 128 : (tile + 1) * 128
            ].astype(jnp.bfloat16)

    def fold(acc, block, land, base, lo, hi):
        for tile, first, end in spans(lo, hi):
            rows = pl.ds(block * 128 + first, end - first)
            acc[rows, tile * 128 : (tile + 1) * 128] += land[
                pl.ds(base + tile * 128 + first - lo, end - first), :
            ].astype(jnp.float32)

    def img_back(move):
        k, slot, _, lo, hi, direction, land = move
        return remote(
            isend.at[pl.ds(slot * D + lo, hi - lo)], iland.at[pl.ds(land, hi - lo)],
            is_s.at[k], is_r.at[k], near[direction],
        )

    def txt_back(move):
        k, slot, _, lo, hi, direction, land = move
        return remote(
            tsend.at[pl.ds(slot * D + lo, hi - lo)], tland.at[pl.ds(land, hi - lo)],
            ts_s.at[k], ts_r.at[k], near[direction],
        )

    def sib_back(k):
        return remote(
            ssend.at[pl.ds(k * D, D)], sland.at[pl.ds(k * D, D)], ss_s.at[k], ss_r.at[k], sib
        )

    def img_give(r):
        for move in IMG_BACK[r]:
            _, slot, _, lo, hi, _, _ = move
            pack(gi, slot, isend, slot * D, lo, hi)
            img_back(move).start()

    def img_add(r):
        for move in IMG_BACK[r]:
            _, _, slot, lo, hi, _, land = move
            img_back(move).wait_recv()
            fold(gi, slot, iland, land, lo, hi)

    def sib_give(r):
        for dz in FRESH[r]:
            k = TPLACE[dz]
            pack(gt, 2 * k + 1, ssend, k * D, 0, D)
            sib_back(k).start()

    def sib_add(r):
        for dz in FRESH[r]:
            k = TPLACE[dz]
            sib_back(k).wait_recv()
            fold(gt, 2 * k, sland, k * D, 0, D)

    def txt_give(r):
        for move in TXT_BACK[r]:
            _, slot, _, lo, hi, _, _ = move
            pack(gt, 2 * slot, tsend, slot * D, lo, hi)
            txt_back(move).start()

    def txt_add(r):
        for move in TXT_BACK[r]:
            _, _, slot, lo, hi, _, land = move
            txt_back(move).wait_recv()
            fold(gt, 2 * slot, tland, land, lo, hi)

    def loss_copies(step):
        buf, me, devices, first = (
            (lc, core, [sib], 0), (lx, x, xs[1:], 1), (ly, y, ys[1:], 4), (lz, z, zs[1:], 7)
        )[step]
        copies = [
            remote(buf.at[me], buf.at[me], l_s.at[first + k], l_r.at[first + k], device)
            for k, device in enumerate(devices)
        ]
        return buf, me, copies

    def loss_give(step, value):
        buf, me, copies = loss_copies(step)
        buf[me] = value
        for copy in copies:
            copy.start()

    def loss_take(step):
        buf, _, copies = loss_copies(step)
        for copy in copies:
            copy.wait_recv()
        return sum(buf[k] for k in range(buf.shape[0]))

    img_start(0)
    txt_start(0)
    gi[...] = jnp.zeros_like(gi)
    gt[...] = jnp.zeros_like(gt)
    total[...] = jnp.zeros_like(total)
    take_img(0, 1)
    take_txt([0], 0)
    sib_wait(0)
    take_txt([0], 1)

    def arrive(r):
        img_wait(r)
        if r < 3:
            img_start(r + 1)
        txt_wait(r)
        txt_start(r + 1)
        first, count = ((1, 4), (5, 6), (11, 4), (15, 1))[r]
        take_img(first, count)
        places = [TPLACE[dz] for dz in FRESH[r + 1]]
        take_txt(places, 0)
        sib_wait(r + 1)
        take_txt(places, 1)

    for r in range(4):
        arrive(r)
    for i0 in (0, 1024):
        for j0 in (0, 1024):
            pairs(i0, 1024, j0, 1024)

    loss_give(0, total[...])
    img_give(3)
    sib_give(4)
    sib_give(3)
    sib_add(4)
    txt_give(3)
    sib_add(3)
    sib_give(2)
    sib_give(1)
    img_add(3)
    img_give(2)
    loss_give(1, loss_take(0))
    txt_add(3)
    txt_give(2)
    sib_give(0)
    sib_add(2)
    sib_add(1)
    sib_add(0)
    loss_give(2, loss_take(1))
    txt_add(2)
    txt_give(1)
    img_add(2)
    img_give(1)
    loss_give(3, loss_take(2))
    txt_add(1)
    txt_give(0)
    img_add(1)
    img_give(0)
    loss_ref[0] = jnp.sum(loss_take(3)) * (math.log(2.0) / BATCH)
    txt_add(0)

    def finish(ref, acc, out):
        unit, norm = unit32(ref)
        grad = acc[pl.ds(0, 128), :] * sharp_ref[0]
        along = jnp.sum(unit * grad, axis=-1, keepdims=True)
        out[...] = ((grad - unit * along) / norm).astype(jnp.bfloat16)

    finish(footage_ref, gt, gtxt_ref)
    img_add(0)
    finish(echo_ref, gi, gimg_ref)

    for r in range(4):
        for move in IMG_OUT[r]:
            img_copy(move).wait_send()
        for move in TXT_OUT[r]:
            txt_copy(move).wait_send()
        for move in IMG_BACK[r]:
            img_back(move).wait_send()
        for move in TXT_BACK[r]:
            txt_back(move).wait_send()
        for copy in loss_copies(r)[2]:
            copy.wait_send()
    for k in range(8):
        sib_copy(k).wait_send()
        sib_back(k).wait_send()


def per_device(echo_vectors, footage_vectors, match_numbers, sharpness_factor, score_offset):
    bf16, f32 = jnp.bfloat16, jnp.float32
    vmem = pl.BlockSpec(memory_space=pltpu.VMEM)
    smem = pl.BlockSpec(memory_space=pltpu.SMEM)
    dma = pltpu.SemaphoreType.DMA
    grad_image, grad_text, loss = pl.pallas_call(
        kernel,
        name="contrastive_step",
        out_shape=[
            jax.ShapeDtypeStruct((ROWS, D), bf16),
            jax.ShapeDtypeStruct((ROWS, D), bf16),
            jax.ShapeDtypeStruct((1,), f32),
        ],
        in_specs=[vmem, vmem, vmem, smem, smem],
        out_specs=[vmem, vmem, smem],
        scratch_shapes=[
            pltpu.VMEM((SLOTS * BLOCK, 128), bf16),
            pltpu.VMEM((SLOTS * BLOCK, 128), bf16),
            pltpu.VMEM((N, D), bf16),
            pltpu.VMEM((N, D), bf16),
            pltpu.VMEM((N, 128), f32),
            pltpu.VMEM((1, N), f32),
            pltpu.VMEM((N, D), f32),
            pltpu.VMEM((N, D), f32),
            pltpu.VMEM((SLOTS * D, 128), bf16),
            pltpu.VMEM((IMG_LAND, 128), bf16),
            pltpu.VMEM((8 * D, 128), bf16),
            pltpu.VMEM((TXT_LAND, 128), bf16),
            pltpu.VMEM((8 * D, 128), bf16),
            pltpu.VMEM((8 * D, 128), bf16),
            pltpu.VMEM((8, 128), f32),
            pltpu.VMEM((2, 8, 128), f32),
            pltpu.VMEM((4, 8, 128), f32),
            pltpu.VMEM((4, 8, 128), f32),
            pltpu.VMEM((8, 8, 128), f32),
            dma((IMG_N,)), dma((IMG_N,)),
            dma((TXT_N,)), dma((TXT_N,)),
            dma((8,)), dma((8,)),
            dma((IMG_N,)), dma((IMG_N,)),
            dma((TXT_N,)), dma((TXT_N,)),
            dma((8,)), dma((8,)),
            dma((14,)), dma((14,)),
        ],
        compiler_params=pltpu.CompilerParams(
            collective_id=0, has_side_effects=True, vmem_limit_bytes=60 << 20
        ),
    )(echo_vectors, footage_vectors, match_numbers.reshape(1, ROWS), sharpness_factor, score_offset)
    return grad_image, grad_text, loss


def solution(mesh):
    return jax.shard_map(
        per_device,
        mesh=mesh,
        in_specs=(
            P(("blk", "inner"), None),
            P(("blk", "inner"), None),
            P(("blk", "inner")),
            P(),
            P(),
        ),
        out_specs=(P(("blk", "inner"), None), P(("blk", "inner"), None), P()),
        check_vma=False,
    )
```

time: 763 us -> 94.2 us (0.12)
  matrix products: 323 us -> 0 us
  starting transfers between devices: 151 us -> 0 us
  blocking collectives: 99.6 us -> 0 us
  Pallas kernels: 0 us -> 86.9 us
  waiting for transfers between devices: 79.5 us -> 0 us
  local copies, waits for them, and re-layouts: 53.5 us -> 2.34 us
  loops' own time: 22.3 us -> 0 us
  between operations: 15.9 us -> 3.76 us
  other arithmetic: 12.1 us -> 0 us
    dot_general x96 -> x0, matrix products: 323 us -> none  [the longest x32 134 us: meet_block(): lax.dot_general(caption_vectors, image_rows, (((1,), (1,)), ((), ())), pr...]
    ppermute x96 -> x0, starting transfers between devices: 151 us -> none  [from_behind(): lax.ppermute(value, axis, [(i, (i + by) % size) for i in range(size)])]
    pallas_call x0 -> x1, Pallas kernels: none -> 86.9 us  [per_device(): pl.pallas_call(kernel, name='contrastive_step', out_shape=[jax.ShapeDtype...]
    psum x1 -> x0, blocking collectives: 78.8 us -> none  [per_device(): loss_all = lax.psum(loss_sum, ('blk', 'inner'))]
    while x192 -> x0, local copies, waits for them, and re-layouts: 51.5 us -> none
    ppermute x96 -> x0, waiting for transfers between devices: 44.3 us -> none  [from_behind(): lax.ppermute(value, axis, [(i, (i + by) % size) for i in range(size)])]
    all_gather x1 -> x0, waiting for transfers between devices: 35.2 us -> none  [per_device(): lax.all_gather(image_unit, 'inner', axis=0, tiled=True)]
    another operation x1 -> x0, loops' own time: 22.3 us -> none  [per_device(): lax.fori_loop(0, cycle_size, advance, start)]
  transfers between devices with their start and end apart: 98 -> 0, of which waited for: 33 -> 0; matrix products, arithmetic and copies ran while one was open for 43% -> 0% of each run, Pallas kernels for 0% -> 0%
where the time goes in v1:
time: 94.2 us; the launch traced here: 93 us
  Pallas kernels  86.9 us (92%)
  between operations  3.76 us (4%)
  local copies, waits for them, and re-layouts  2.34 us (2%)
    pallas_call x1, Pallas kernels, per_device(): pl.pallas_call(kernel, name='contrastive_step', out_shape=[jax.ShapeDtype...  86.9 us
    unnamed x4, local copies, waits for them, and re-layouts  2.34 us

profile of v1, /device:TPU:1, one launch (start us, length us, event | category | flops | bytes accessed | tf_op | source)
XLA Modules:
  0.0 93.0 jit_solution(8774306031836571722)
XLA Ops:
  1.9 86.9 %contrastive_step.1 = (bf16[128,768]{1,0:T(8,128)(2,1)}, bf16[128,768]{1,0:T(8,128)(2,1)}, f32[1]{0:T(128)}) custom-call(bf16[128,768]{1,0:T(8,128)(2,1)} %echo_ref.1, bf16[128,768]{1,0:T(8,128)(2,1)} %footage_ref.1, s32[1,128]{1,0:T(1,128)} %bitcast.1, f32[1]{0:T(128)S(6)} %copy.11.sharp_ref, f32[1]{0:T(128)S(6)} %copy.12.offset_ref), custom_call_target="tpu_custom_call" | custom-call | tf_op jit(solution)/shard_map/contrastive_step/pallas_call | solution.py:421
  88.8 0.0 copy-start
  88.9 1.7 %copy.13 = bf16[128,768]{1,0:T(8,128)(2,1)} copy(bf16[128,768]{1,0:T(8,128)(2,1)} %get-tuple-element.6) | data formatting | bytes 393216
  90.5 0.0 copy-done
  90.5 0.7 copy.14
Async XLA Ops:
  88.8 1.7 %copy-start = (bf16[128,768]{1,0:T(8,128)(2,1)S(1)}, bf16[128,768]{1,0:T(8,128)(2,1)}, u32[]{:S(2)}) copy-start(bf16[128,768]{1,0:T(8,128)(2,1)} %get-tuple-element.7) | copy-start | bytes 589828

commit v2 on v1

--- a/solution.py
+++ b/solution.py
@@ -16,7 +16,7 @@
 BATCH = 32768
 MESH = pl.DeviceIdType.MESH
 
-WHOLE, A, B = (0, BLOCK), (0, 384), (384, BLOCK)
+A, B = (0, 384), (384, BLOCK)
 A0, A1, B0, B1 = (0, 192), (192, 384), (384, 576), (576, BLOCK)
 
 PLACES = [
@@ -28,28 +28,41 @@
 STEP = {"+x": (1, 0), "-x": (3, 0), "+y": (0, 1), "-y": (0, 3)}
 BACK = {"+x": "-x", "-x": "+x", "+y": "-y", "-y": "+y", "+z": "-z", "-z": "+z"}
 IMG = [
-    [((0, 0), WHOLE, d) for d in ("+x", "-x", "+y", "-y")],
     [
-        ((0, 1), B, "+x"), ((0, 1), B, "-x"), ((1, 0), A, "+y"), ((1, 0), A, "-y"),
-        ((0, 3), B, "+x"), ((0, 3), B, "-x"), ((3, 0), A, "+y"), ((3, 0), A, "-y"),
-        ((3, 0), A, "+x"), ((1, 0), B, "-x"), ((0, 3), A, "+y"), ((0, 1), B, "-y"),
+        ((0, 0), A, "+x"), ((0, 0), A, "-x"), ((0, 0), B, "+y"), ((0, 0), B, "-y"),
+        ((0, 0), B, "+x"), ((0, 0), B, "-x"), ((0, 0), A, "+y"), ((0, 0), A, "-y"),
+    ],
+    [
+        ((3, 0), A, "+x"), ((0, 1), B, "-x"), ((1, 0), A, "+y"), ((0, 1), B, "-y"),
+        ((0, 1), B, "+x"), ((1, 0), A, "-y"),
+    ],
+    [
+        ((1, 0), B, "-x"), ((0, 3), A, "+y"), ((0, 3), B, "+x"), ((3, 0), A, "-y"),
+        ((0, 3), B, "-x"), ((3, 0), A, "+y"),
     ],
     [
         ((0, 2), B, "+x"), ((0, 2), B, "-x"), ((2, 0), A, "+y"), ((2, 0), A, "-y"),
-        ((3, 1), B0, "+x"), ((1, 1), B1, "-x"), ((1, 3), A0, "+y"), ((1, 1), A1, "-y"),
-        ((3, 3), B0, "+x"), ((1, 3), B1, "-x"), ((3, 3), A0, "+y"), ((3, 1), A1, "-y"),
+        ((1, 1), B1, "-x"), ((1, 3), A0, "+y"),
     ],
+    [((3, 1), B0, "+x"), ((1, 1), A1, "-y")],
+    [((3, 3), B0, "+x"), ((1, 3), B1, "-x"), ((3, 3), A0, "+y"), ((3, 1), A1, "-y")],
     [((3, 2), B0, "+x"), ((1, 2), B1, "-x"), ((2, 3), A0, "+y"), ((2, 1), A1, "-y")],
 ]
 DZ = [0, 1, 7, 2, 6, 3, 5, 4]
 TPLACE = {dz: k for k, dz in enumerate(DZ)}
+TORDER = [
+    (0, 0), (0, 1), (1, 0), (7, 0), (1, 1), (7, 1), (2, 0), (6, 0), (2, 1), (6, 1),
+    (3, 0), (5, 0), (3, 1), (5, 1), (4, 0), (4, 1),
+]
+TSLOT = {place: slot for slot, place in enumerate(TORDER)}
 TXT = [
-    [(0, WHOLE, "+z"), (0, WHOLE, "-z")],
-    [(7, WHOLE, "+z"), (1, WHOLE, "-z")],
-    [(6, WHOLE, "+z"), (2, WHOLE, "-z")],
+    [(0, A, "+z"), (0, B, "-z"), (0, B, "+z"), (0, A, "-z")],
+    [(7, A, "+z"), (1, B, "-z")],
+    [(7, B, "+z"), (1, A, "-z")],
+    [(6, A, "+z"), (2, B, "-z")],
+    [(6, B, "+z"), (2, A, "-z")],
     [(5, A, "+z"), (3, B, "-z")],
 ]
-FRESH = [[0], [1, 7], [2, 6], [3, 5], [4]]
 
 
 def img_to(place, direction):
@@ -82,13 +95,19 @@
 
 
 def spans(lo, hi):
-    parts = []
-    while lo < hi:
-        tile = lo // 128
-        end = min(hi, (tile + 1) * 128)
-        parts.append((tile, lo - tile * 128, end - tile * 128))
-        lo = end
-    return parts
+    edges = [e for e in range(0, D + 1, 64) if lo <= e <= hi and (e % 128 == 0 or e % 192 == 0)]
+    return list(zip(edges[:-1], edges[1:]))
+
+
+def incoming(rounds):
+    found = {}
+    for moves in rounds:
+        for _, _, slot, lo, hi, _, land in moves:
+            found.setdefault(slot, []).append((lo, hi, land))
+    return found
+
+
+IMG_IN, TXT_IN = incoming(IMG_BACK), incoming(TXT_BACK)
 
 
 def kernel(
@@ -167,27 +186,20 @@
             sg_s.at[k], sg_r.at[k], sib,
         )
 
-    def img_start(r):
-        for move in IMG_OUT[r]:
-            img_copy(move).start()
-
-    def img_wait(r):
-        for move in IMG_OUT[r]:
-            img_copy(move).wait_recv()
-
-    def txt_start(r):
-        if r < 4:
-            for move in TXT_OUT[r]:
-                txt_copy(move).start()
-        for dz in FRESH[r]:
+    def start(copy, moves):
+        for move in moves:
+            copy(move).start()
+
+    def arrived(copy, moves):
+        for move in moves:
+            copy(move).wait_recv()
+
+    def sib_start(*places):
+        for dz in places:
             sib_copy(TPLACE[dz]).start()
 
-    def txt_wait(r):
-        for move in TXT_OUT[r]:
-            txt_copy(move).wait_recv()
-
-    def sib_wait(r):
-        for dz in FRESH[r]:
+    def sib_wait(*places):
+        for dz in places:
             sib_copy(TPLACE[dz]).wait_recv()
 
     def ids_of(slots, base):
@@ -204,9 +216,9 @@
             return carry
         lax.fori_loop(first, first + count, body, 0)
 
-    def take_txt(places, lane):
-        for k in places:
-            slot = 2 * k + lane
+    def take_txt(lane, *places):
+        for dz in places:
+            k, slot = TPLACE[dz], TSLOT[dz, lane]
             base = (8 * lane + k) * BLOCK
             for c in range(TILES):
                 txt[slot * 128 : (slot + 1) * 128, c * 128 : (c + 1) * 128] = trx[
@@ -237,18 +249,29 @@
             preferred_element_type=jnp.float32,
         )
 
-    def pack(acc, block, out, base, lo, hi):
-        for tile, first, end in spans(lo, hi):
-            out[pl.ds(base + tile * 128 + first, end - first), :] = acc[
-                pl.ds(block * 128 + first, end - first), tile * 128 : (tile + 1) * 128
-            ].astype(jnp.bfloat16)
-
-    def fold(acc, block, land, base, lo, hi):
-        for tile, first, end in spans(lo, hi):
-            rows = pl.ds(block * 128 + first, end - first)
-            acc[rows, tile * 128 : (tile + 1) * 128] += land[
-                pl.ds(base + tile * 128 + first - lo, end - first), :
-            ].astype(jnp.float32)
+    def summed(acc, block, lo, hi, lands):
+        tile, first = lo // 128, lo % 128
+        value = acc[
+            pl.ds(block * 128 + first, hi - lo), tile * 128 : (tile + 1) * 128
+        ]
+        for land, base, top, end in lands:
+            if top <= lo and hi <= end:
+                value = value + land[pl.ds(base + lo - top, hi - lo), :].astype(jnp.float32)
+        return value
+
+    def img_lands(slot):
+        return [(iland, base, lo, hi) for lo, hi, base in IMG_IN.get(slot, [])]
+
+    def txt_lands(k):
+        return [(sland, k * D, 0, D)] + [
+            (tland, base, lo, hi) for lo, hi, base in TXT_IN.get(k, [])
+        ]
+
+    def pack(acc, block, out, base, lo, hi, lands):
+        for first, end in spans(lo, hi):
+            out[pl.ds(base + first, end - first), :] = summed(
+                acc, block, first, end, lands
+            ).astype(jnp.bfloat16)
 
     def img_back(move):
         k, slot, _, lo, hi, direction, land = move
@@ -269,41 +292,27 @@
             ssend.at[pl.ds(k * D, D)], sland.at[pl.ds(k * D, D)], ss_s.at[k], ss_r.at[k], sib
         )
 
-    def img_give(r):
-        for move in IMG_BACK[r]:
+    def img_give(moves):
+        for move in moves:
             _, slot, _, lo, hi, _, _ = move
-            pack(gi, slot, isend, slot * D, lo, hi)
+            pack(gi, slot, isend, slot * D, lo, hi, img_lands(slot))
             img_back(move).start()
 
-    def img_add(r):
-        for move in IMG_BACK[r]:
-            _, _, slot, lo, hi, _, land = move
-            img_back(move).wait_recv()
-            fold(gi, slot, iland, land, lo, hi)
-
-    def sib_give(r):
-        for dz in FRESH[r]:
+    def sib_give(*places):
+        for dz in places:
             k = TPLACE[dz]
-            pack(gt, 2 * k + 1, ssend, k * D, 0, D)
+            pack(gt, TSLOT[dz, 1], ssend, k * D, 0, D, [])
             sib_back(k).start()
 
-    def sib_add(r):
-        for dz in FRESH[r]:
-            k = TPLACE[dz]
-            sib_back(k).wait_recv()
-            fold(gt, 2 * k, sland, k * D, 0, D)
-
-    def txt_give(r):
-        for move in TXT_BACK[r]:
-            _, slot, _, lo, hi, _, _ = move
-            pack(gt, 2 * slot, tsend, slot * D, lo, hi)
+    def sib_got(*places):
+        for dz in places:
+            sib_back(TPLACE[dz]).wait_recv()
+
+    def txt_give(moves):
+        for move in moves:
+            _, k, _, lo, hi, _, _ = move
+            pack(gt, TSLOT[DZ[k], 0], tsend, k * D, lo, hi, txt_lands(k))
             txt_back(move).start()
-
-    def txt_add(r):
-        for move in TXT_BACK[r]:
-            _, _, slot, lo, hi, _, land = move
-            txt_back(move).wait_recv()
-            fold(gt, 2 * slot, tland, land, lo, hi)
 
     def loss_copies(step):
         buf, me, devices, first = (
@@ -327,85 +336,152 @@
             copy.wait_recv()
         return sum(buf[k] for k in range(buf.shape[0]))
 
-    img_start(0)
-    txt_start(0)
+    I, T, IB, TB = IMG_OUT, TXT_OUT, IMG_BACK, TXT_BACK
+    start(img_copy, I[0][:4])
+    start(txt_copy, T[0][:2])
+    start(img_copy, I[0][4:])
+    start(txt_copy, T[0][2:])
+    sib_start(0)
     gi[...] = jnp.zeros_like(gi)
     gt[...] = jnp.zeros_like(gt)
     total[...] = jnp.zeros_like(total)
     take_img(0, 1)
-    take_txt([0], 0)
+    take_txt(0, 0)
+
+    arrived(img_copy, I[0][:4])
+    start(img_copy, I[1])
+    arrived(txt_copy, T[0][:2])
+    start(txt_copy, T[1])
     sib_wait(0)
-    take_txt([0], 1)
-
-    def arrive(r):
-        img_wait(r)
-        if r < 3:
-            img_start(r + 1)
-        txt_wait(r)
-        txt_start(r + 1)
-        first, count = ((1, 4), (5, 6), (11, 4), (15, 1))[r]
-        take_img(first, count)
-        places = [TPLACE[dz] for dz in FRESH[r + 1]]
-        take_txt(places, 0)
-        sib_wait(r + 1)
-        take_txt(places, 1)
-
-    for r in range(4):
-        arrive(r)
-    for i0 in (0, 1024):
-        for j0 in (0, 1024):
-            pairs(i0, 1024, j0, 1024)
-
+    take_txt(1, 0)
+
+    arrived(img_copy, I[0][4:])
+    start(img_copy, I[2])
+    arrived(txt_copy, T[0][2:])
+    start(txt_copy, T[2])
+    sib_start(1, 7)
+    take_img(1, 4)
+    take_txt(0, 1, 7)
+    pairs(0, 640, 0, 512)
+
+    arrived(img_copy, I[1][:4])
+    start(img_copy, I[3])
+    arrived(txt_copy, T[1])
+    start(txt_copy, T[3])
+    sib_wait(1, 7)
+    take_txt(1, 1, 7)
+    pairs(0, 640, 512, 256)
+
+    arrived(img_copy, I[1][4:])
+    start(img_copy, I[4])
+    arrived(txt_copy, T[2])
+    start(txt_copy, T[4])
+    sib_start(2, 6)
+    take_txt(0, 2, 6)
+    pairs(0, 640, 768, 256)
+
+    arrived(img_copy, I[2])
+    start(img_copy, I[5])
+    arrived(txt_copy, T[3])
+    start(txt_copy, T[5])
+    take_img(5, 6)
+    pairs(640, 768, 0, 512)
+
+    arrived(img_copy, I[3][:4])
+    start(img_copy, I[6])
+    arrived(txt_copy, T[4])
+    sib_start(3, 5)
+    sib_wait(2, 6)
+    take_txt(1, 2, 6)
+    pairs(640, 768, 512, 512)
+
+    arrived(txt_copy, T[5])
+    sib_start(4)
+    pairs(0, 1408, 1024, 256)
+
+    for moves in (I[3][4:], I[4], I[5], I[6]):
+        arrived(img_copy, moves)
+    take_img(11, 5)
+    pairs(1408, 640, 0, 1280)
+    take_txt(0, 3, 5, 4)
+    sib_wait(3, 5, 4)
+    take_txt(1, 3, 5, 4)
+    sib_give(2, 6, 1, 7, 0)
+    pairs(1408, 640, 1280, 768)
+    img_give(IB[6])
+    for moves in (IB[5], IB[4], IB[3][4:]):
+        img_give(moves)
+    pairs(0, 1408, 1792, 256)
+    sib_give(4)
+    sib_got(2, 6, 1, 7, 0)
+    pairs(640, 768, 1280, 512)
+    arrived(img_back, IB[6])
+    img_give(IB[3][:4])
+    for moves in (IB[5], IB[4], IB[3][4:]):
+        arrived(img_back, moves)
+    first = [IB[1][1], IB[2][2], IB[2][3], IB[1][2], IB[2][4], IB[1][4], IB[1][5], IB[2][5]]
+    third = [IB[2][0], IB[2][1]]
+    late = [IB[1][0], IB[1][3]]
+    img_give(first)
+    img_give(third)
+    sib_got(4)
+    txt_give(TB[5])
+    pairs(0, 640, 1280, 512)
+
+    sib_give(3, 5)
     loss_give(0, total[...])
-    img_give(3)
-    sib_give(4)
-    sib_give(3)
-    sib_add(4)
-    txt_give(3)
-    sib_add(3)
-    sib_give(2)
-    sib_give(1)
-    img_add(3)
-    img_give(2)
+    home = {(slot, lo): move for move in IB[0] for _, slot, _, lo, _, _, _ in [move]}
+    arrived(img_back, IB[3][:4])
+    img_give(late)
+    img_give([home[2, 384], home[3, 0]])
+    sib_got(3, 5)
+    txt_give(TB[4])
+    arrived(txt_back, TB[5])
+    txt_give(TB[3])
     loss_give(1, loss_take(0))
-    txt_add(3)
-    txt_give(2)
-    sib_give(0)
-    sib_add(2)
-    sib_add(1)
-    sib_add(0)
+    arrived(img_back, first)
+    img_give([home[1, 0], home[4, 384]])
+    arrived(txt_back, TB[4])
+    txt_give(TB[2])
     loss_give(2, loss_take(1))
-    txt_add(2)
-    txt_give(1)
-    img_add(2)
-    img_give(1)
+    arrived(img_back, third)
+    img_give([home[1, 384], home[4, 0]])
+    arrived(txt_back, TB[3])
+    txt_give(TB[1])
+    arrived(img_back, late)
+    img_give([home[2, 0], home[3, 384]])
     loss_give(3, loss_take(2))
-    txt_add(1)
-    txt_give(0)
-    img_add(1)
-    img_give(0)
+    arrived(txt_back, TB[2])
+    txt_give(TB[0][2:])
+    arrived(txt_back, TB[1])
+    txt_give(TB[0][:2])
     loss_ref[0] = jnp.sum(loss_take(3)) * (math.log(2.0) / BATCH)
-    txt_add(0)
-
-    def finish(ref, acc, out):
+
+    def finish(ref, acc, lands, out):
         unit, norm = unit32(ref)
-        grad = acc[pl.ds(0, 128), :] * sharp_ref[0]
+        tiles = [summed(acc, 0, c * 128, (c + 1) * 128, lands) for c in range(TILES)]
+        grad = jnp.concatenate(tiles, axis=1) * sharp_ref[0]
         along = jnp.sum(unit * grad, axis=-1, keepdims=True)
         out[...] = ((grad - unit * along) / norm).astype(jnp.bfloat16)
 
-    finish(footage_ref, gt, gtxt_ref)
-    img_add(0)
-    finish(echo_ref, gi, gimg_ref)
-
+    arrived(img_back, IB[0])
+    finish(echo_ref, gi, img_lands(0), gimg_ref)
+    arrived(txt_back, TB[0])
+    finish(footage_ref, gt, txt_lands(0), gtxt_ref)
+
+    for moves in I:
+        for move in moves:
+            img_copy(move).wait_send()
+    for moves in T:
+        for move in moves:
+            txt_copy(move).wait_send()
+    for moves in IB:
+        for move in moves:
+            img_back(move).wait_send()
+    for moves in TB:
+        for move in moves:
+            txt_back(move).wait_send()
     for r in range(4):
-        for move in IMG_OUT[r]:
-            img_copy(move).wait_send()
-        for move in TXT_OUT[r]:
-            txt_copy(move).wait_send()
-        for move in IMG_BACK[r]:
-            img_back(move).wait_send()
-        for move in TXT_BACK[r]:
-            txt_back(move).wait_send()
         for copy in loss_copies(r)[2]:
             copy.wait_send()
     for k in range(8):

time: 94.2 us -> 82 us (0.87)
  Pallas kernels: 86.9 us -> 74.3 us
    pallas_call x1, Pallas kernels: 86.9 us -> 74.3 us  [per_device(): pl.pallas_call(kernel, name='contrastive_step', out_shape=[jax.ShapeDtype...]
where the time goes in v2:
time: 82 us; the launch traced here: 80.4 us
  Pallas kernels  74.3 us (91%)
  between operations  3.76 us (5%)
  local copies, waits for them, and re-layouts  2.34 us (3%)
    pallas_call x1, Pallas kernels, per_device(): pl.pallas_call(kernel, name='contrastive_step', out_shape=[jax.ShapeDtype...  74.3 us
    unnamed x4, local copies, waits for them, and re-layouts  2.34 us

profile of v2, /device:TPU:1, one launch (start us, length us, event | category | flops | bytes accessed | tf_op | source)
XLA Modules:
  0.0 80.4 jit_solution(992899911775655358)
XLA Ops:
  1.9 74.3 %contrastive_step.1 = (bf16[128,768]{1,0:T(8,128)(2,1)}, bf16[128,768]{1,0:T(8,128)(2,1)}, f32[1]{0:T(128)}) custom-call(bf16[128,768]{1,0:T(8,128)(2,1)} %echo_ref.1, bf16[128,768]{1,0:T(8,128)(2,1)} %footage_ref.1, s32[1,128]{1,0:T(1,128)} %bitcast.1, f32[1]{0:T(128)S(6)} %copy.11.sharp_ref, f32[1]{0:T(128)S(6)} %copy.12.offset_ref), custom_call_target="tpu_custom_call" | custom-call | tf_op jit(solution)/shard_map/contrastive_step/pallas_call | solution.py:497
  76.2 0.0 copy-start
  76.3 1.7 %copy.13 = bf16[128,768]{1,0:T(8,128)(2,1)} copy(bf16[128,768]{1,0:T(8,128)(2,1)} %get-tuple-element.6) | data formatting | bytes 393216
  77.9 0.0 copy-done
  77.9 0.7 copy.14
Async XLA Ops:
  76.2 1.7 %copy-start = (bf16[128,768]{1,0:T(8,128)(2,1)S(1)}, bf16[128,768]{1,0:T(8,128)(2,1)}, u32[]{:S(2)}) copy-start(bf16[128,768]{1,0:T(8,128)(2,1)} %get-tuple-element.7) | copy-start | bytes 589828

commit v3 on v2

--- a/solution.py
+++ b/solution.py
@@ -138,7 +138,7 @@
     near = {"+x": xs[1], "-x": xs[3], "+y": ys[1], "-y": ys[3], "+z": zs[1], "-z": zs[7]}
 
     barrier = pltpu.get_barrier_semaphore()
-    partners = xs[1:] + ys[1:] + zs[1:] + [sib]
+    partners = list(near.values()) + [sib]
     for device in partners:
         pl.semaphore_signal(barrier, inc=1, device_id=device, device_id_type=MESH)
 
@@ -152,12 +152,13 @@
     high = jnp.broadcast_to((ids >> 6).astype(jnp.float32), (16, 128))
     low = jnp.broadcast_to((ids & 63).astype(jnp.float32), (16, 128))
     id_rows = jnp.where(row == 0, high, jnp.where(row == 1, low, 0.0)).astype(jnp.bfloat16)
-    for ref, slots in ((echo_ref, irx), (footage_ref, trx)):
+    def place_own(ref, slots):
         unit = unit32(ref)[0].astype(jnp.bfloat16)
         for c in range(TILES):
             slots[pl.ds(c * 128, 128), :] = unit[:, c * 128 : (c + 1) * 128]
         slots[pl.ds(D, 16), :] = id_rows
 
+    place_own(echo_ref, irx)
     pl.semaphore_wait(barrier, len(partners))
 
     def remote(src, dst, send, recv, device):
@@ -338,6 +339,7 @@
 
     I, T, IB, TB = IMG_OUT, TXT_OUT, IMG_BACK, TXT_BACK
     start(img_copy, I[0][:4])
+    place_own(footage_ref, trx)
     start(txt_copy, T[0][:2])
     start(img_copy, I[0][4:])
     start(txt_copy, T[0][2:])
@@ -455,7 +457,9 @@
     txt_give(TB[0][2:])
     arrived(txt_back, TB[1])
     txt_give(TB[0][:2])
-    loss_ref[0] = jnp.sum(loss_take(3)) * (math.log(2.0) / BATCH)
+    loss_ref[...] = jnp.broadcast_to(
+        jnp.sum(loss_take(3), keepdims=True) * (math.log(2.0) / BATCH), (8, 128)
+    )
 
     def finish(ref, acc, lands, out):
         unit, norm = unit32(ref)
@@ -500,10 +504,10 @@
         out_shape=[
             jax.ShapeDtypeStruct((ROWS, D), bf16),
             jax.ShapeDtypeStruct((ROWS, D), bf16),
-            jax.ShapeDtypeStruct((1,), f32),
+            jax.ShapeDtypeStruct((8, 128), f32),
         ],
         in_specs=[vmem, vmem, vmem, smem, smem],
-        out_specs=[vmem, vmem, smem],
+        out_specs=[vmem, vmem, vmem],
         scratch_shapes=[
             pltpu.VMEM((SLOTS * BLOCK, 128), bf16),
             pltpu.VMEM((SLOTS * BLOCK, 128), bf16),
@@ -536,7 +540,7 @@
             collective_id=0, has_side_effects=True, vmem_limit_bytes=60 << 20
         ),
     )(echo_vectors, footage_vectors, match_numbers.reshape(1, ROWS), sharpness_factor, score_offset)
-    return grad_image, grad_text, loss
+    return grad_image, grad_text, loss[0, :1]
 
 
 def solution(mesh):

time: 82 us -> 80.2 us (0.978); the launches traced: 80.4 us -> 80 us
  between operations: 3.76 us -> 1.93 us
  local copies, waits for them, and re-layouts: 2.34 us -> 3.53 us
    slice x0 -> x1, local copies, waits for them, and re-layouts: none -> 1.19 us  [per_device(): return (grad_image, grad_text, loss[0, :1])]
where the time goes in v3:
time: 80.2 us; the launch traced here: 80 us
  Pallas kernels  74.6 us (93%)
  local copies, waits for them, and re-layouts  3.53 us (4%)
  between operations  1.93 us (2%)
    pallas_call x1, Pallas kernels, per_device(): pl.pallas_call(kernel, name='contrastive_step', out_shape=[jax.ShapeDtype...  74.6 us
    unnamed x4, local copies, waits for them, and re-layouts  2.34 us

profile of v3, /device:TPU:1, one launch (start us, length us, event | category | flops | bytes accessed | tf_op | source)
XLA Modules:
  0.0 80.0 jit_solution(2498816291020917931)
XLA Ops:
  1.9 74.6 %contrastive_step.1 = (bf16[128,768]{1,0:T(8,128)(2,1)}, bf16[128,768]{1,0:T(8,128)(2,1)}, f32[8,128]{1,0:T(8,128)}) custom-call(bf16[128,768]{1,0:T(8,128)(2,1)} %echo_ref.1, bf16[128,768]{1,0:T(8,128)(2,1)} %footage_ref.1, s32[1,128]{1,0:T(1,128)} %bitcast.2, f32[1]{0:T(128)S(6)} %copy.10.sharp_ref, f32[1]{0:T(128)S(6)} %copy.11.offset_ref), custom_call_target="tpu_custom_call" | custom-call | tf_op jit(solution)/shard_map/contrastive_step/pallas_call | solution.py:501
  76.5 1.2 %slice.3 = f32[1,1]{1,0:T(1,128)} slice(f32[8,128]{1,0:T(8,128)} %get-tuple-element.8), slice={[0:1], [0:1]} | slice | bytes 8 | tf_op jit(solution)/shard_map/slice | solution.py:543
  77.7 0.0 copy-start
  77.7 1.7 %copy.12 = bf16[128,768]{1,0:T(8,128)(2,1)} copy(bf16[128,768]{1,0:T(8,128)(2,1)} %get-tuple-element.12) | data formatting | bytes 393216
  79.3 0.0 copy-done
  79.3 0.7 copy.13
Async XLA Ops:
  77.7 1.7 %copy-start = (bf16[128,768]{1,0:T(8,128)(2,1)S(1)}, bf16[128,768]{1,0:T(8,128)(2,1)}, u32[]{:S(2)}) copy-start(bf16[128,768]{1,0:T(8,128)(2,1)} %get-tuple-element.13) | copy-start | bytes 589828
